TPU v7x, 32 devices: a whole 2x2x4 slice. The times are simulated.
32 devices in a mesh: groups: 2 (over y), ctx: 4 (over z), dp: 2 (over x), mp: 2 (over core).
Axes of the slice: x: 2, y: 2, z: 4, core: 2. Of those that a mesh axis runs over, the one named last changes fastest.
Arguments:
- head_inputs: bfloat16 [3, 4, 1024, 1536], P(None, ('groups', 'dp'), 'ctx', 'mp'), parts along dimension 1, may hold values from -0.29882812 to 0.29882812
- write_read: bfloat16 [3, 4, 1024, 128], P(None, ('groups', 'dp'), 'ctx'), parts along dimension 1, may hold values from -0.26953125 to 0.26953125
- decay_steps: int32 [3, 4, 12, 1024], P(None, ('groups', 'dp'), 'mp', 'ctx'), parts along dimension 1, may hold values from 0 to 512
- scan_orders: int32 [2, 4, 1024], P(None, ('groups', 'dp'), 'ctx'), parts along dimension 1, may hold values from 0 to 1023, as said below
- cotangent: bfloat16 [4, 1024, 768], P(('groups', 'dp'), 'ctx'), parts along dimension 0, may hold values from -0.59765625 to 0.59765625
- out_weight: bfloat16 [3, 768, 1536], P(None, 'ctx', 'mp'), may hold values from -0.4375 to 0.4375
Outputs:
- grad_inputs: bfloat16 [3, 4, 1024, 1536], P(None, ('groups', 'dp'), 'ctx', 'mp'), parts along dimension 1
- grad_write_read: bfloat16 [3, 4, 1024, 128], P(None, ('groups', 'dp'), 'ctx'), parts along dimension 1
- grad_weight: bfloat16 [6, 768, 1536], P('groups', 'ctx', 'mp'), parts along dimension 0
There are 2 independent parts, one for each index of `groups`. A program takes and returns all parts, laid end to end along the dimension named above; an argument that names none is the same for every part. Nothing has to cross between parts.
Inputs may be any that keep to these rules, and one draw needn't show every extreme that they name: `scan_orders`: for every volume and each of the two orders, position d * 256 + q * 64 + m (0 <= m < 64) holds a patch of index q * 256 + d * 64 + m' with 0 <= m' < 64; every patch stands at exactly one position.
All inputs are finite; a program needn't handle non-finite values.
Results may differ from a plain program's by a relative error of at most 0.005.
Values may be sent and summed in bfloat16 or wider, within the bound.
A program may use at most 128 MiB of HBM per device.

v0:
```python
import math
import jax
import jax.numpy as jnp
from jax import lax
from jax.sharding import PartitionSpec as P

P_SIZE = 128
N = 64
EXACT = lax.Precision.HIGHEST


def prefix(value, axis, join, neutral, backward):
    count, mine = (lax.axis_size(axis), lax.axis_index(axis))
    pieces = jax.tree.map(lambda part: lax.all_gather(part, axis), value)
    if backward:
        pieces = jax.tree.map(lambda part: part[::-1], pieces)
        mine = count - 1 - mine
    running = jax.tree.map(
        lambda part, zero: jnp.full_like(part, 0) + jnp.asarray(zero, part.dtype), value, neutral
    )

    def lap(position, running):
        longer = join(running, jax.tree.map(lambda part: part[position], pieces))
        return jax.tree.map(lambda new, old: jnp.where(position < mine, new, old), longer, running)

    return lax.fori_loop(0, count - 1, lap, running)


def contract(form, *operands):
    return jnp.einsum(form, *operands, precision=EXACT)


def segment_parts(log_rates, writes, readers):
    running = jnp.cumsum(log_rates, axis=-1)
    final_log = running[..., -1]
    length = log_rates.shape[-1]
    causal = jnp.arange(length)[:, None] >= jnp.arange(length)[None, :]
    differ = jnp.where(causal, running[..., :, None] - running[..., None, :], 0.0)
    decay_mat = jnp.where(causal, jnp.exp(differ), 0.0)
    scores = contract("ovin,ovjn->ovij", readers, writes)
    mixing = scores[:, :, None] * decay_mat
    return (running, final_log, decay_mat, mixing)


def segment_forward(pieces, signal, writes, readers, memory):
    running, final_log, decay_mat, mixing = pieces
    rising = jnp.exp(running)
    falling = jnp.exp(final_log[..., None] - running)
    outputs = contract("ovhij,ovjhp->ovihp", mixing, signal) + contract(
        "ovhi,ovin,ovhnp->ovihp", rising, readers, memory
    )
    memory_next = jnp.exp(final_log)[..., None, None] * memory + contract(
        "ovhj,ovjn,ovjhp->ovhnp", falling, writes, signal
    )
    return (outputs, memory_next)


def segment_backward(pieces, signal, writes, readers, upstream, memory, memory_grad):
    running, final_log, decay_mat, mixing = pieces
    rising = jnp.exp(running)
    falling = jnp.exp(final_log[..., None] - running)
    grad_signal = contract("ovhij,ovihp->ovjhp", mixing, upstream) + contract(
        "ovhj,ovjn,ovhnp->ovjhp", falling, writes, memory_grad
    )
    weighted = contract("ovihp,ovjhp->ovhij", upstream, signal) * decay_mat
    grad_writes = contract("ovhij,ovin->ovjn", weighted, readers) + contract(
        "ovhj,ovjhp,ovhnp->ovjn", falling, signal, memory_grad
    )
    grad_readers = contract("ovhij,ovjn->ovin", weighted, writes) + contract(
        "ovhi,ovihp,ovhnp->ovin", rising, upstream, memory
    )
    grad_prev = jnp.exp(final_log)[..., None, None] * memory_grad + contract(
        "ovhi,ovin,ovihp->ovhnp", rising, readers, upstream
    )
    return (grad_signal, grad_writes, grad_readers, grad_prev)


def run_segments(signal, writes, readers, log_rates, upstream, memory_in, grad_in, length):
    blocks = signal.shape[2] // length

    def cut_rows(array, number, along):
        start_row = (number * length).astype(jnp.int32)
        return lax.dynamic_slice_in_dim(array, start_row, length, along)

    def forward_turn(number, carried):
        memory, outputs, memories = carried
        sig = cut_rows(signal, number, 2)
        wri = cut_rows(writes, number, 2)
        rea = cut_rows(readers, number, 2)
        pieces = segment_parts(cut_rows(log_rates, number, 3), wri, rea)
        out_rows, memory_next = segment_forward(pieces, sig, wri, rea, memory)
        outputs = lax.dynamic_update_slice_in_dim(
            outputs, out_rows, (number * length).astype(jnp.int32), 2
        )
        memories = lax.dynamic_update_index_in_dim(memories, memory, number, 0)
        return (memory_next, outputs, memories)

    start_memories = jnp.zeros((blocks,) + memory_in.shape, memory_in.dtype)
    _, outputs, memories = lax.fori_loop(
        0, blocks, forward_turn, (memory_in, jnp.zeros_like(signal), start_memories)
    )

    def backward_turn(countdown, carried):
        memory_grad, grad_signal, grad_writes, grad_readers = carried
        number = blocks - 1 - countdown
        sig = cut_rows(signal, number, 2)
        wri = cut_rows(writes, number, 2)
        rea = cut_rows(readers, number, 2)
        pieces = segment_parts(cut_rows(log_rates, number, 3), wri, rea)
        memory = lax.dynamic_index_in_dim(memories, number, 0, keepdims=False)
        part_sig, part_wri, part_rea, grad_prev = segment_backward(
            pieces, sig, wri, rea, cut_rows(upstream, number, 2), memory, memory_grad
        )
        start_row = (number * length).astype(jnp.int32)
        grad_signal = lax.dynamic_update_slice_in_dim(grad_signal, part_sig, start_row, 2)
        grad_writes = lax.dynamic_update_slice_in_dim(grad_writes, part_wri, start_row, 2)
        grad_readers = lax.dynamic_update_slice_in_dim(grad_readers, part_rea, start_row, 2)
        return (grad_prev, grad_signal, grad_writes, grad_readers)

    _, grad_signal, grad_writes, grad_readers = lax.fori_loop(
        0,
        blocks,
        backward_turn,
        (grad_in, jnp.zeros_like(signal), jnp.zeros_like(writes), jnp.zeros_like(readers)),
    )
    return (outputs, grad_signal, grad_writes, grad_readers)


def carry_forward(earlier, later):
    return (earlier[0] + later[0], jnp.exp(later[0])[..., None, None] * earlier[1] + later[1])


def carry_backward(earlier, later):
    return (earlier[0] + later[0], later[1] + jnp.exp(later[0])[..., None, None] * earlier[1])


def shards(head_inputs, write_read, decay_steps, scan_orders, cotangent, out_weight):
    volumes, tokens, model_width = cotangent.shape
    ctx_count = lax.axis_size("ctx")
    seq_len = tokens * ctx_count
    local_heads = decay_steps.shape[2]
    inner_width = head_inputs.shape[3]
    gathered = lax.all_gather(cotangent, "ctx", axis=1, tiled=True)

    def reorder(ordering):
        return jax.vmap(lambda table_rows, row_ids: table_rows[row_ids])(gathered, ordering)

    scanned = jnp.stack([cotangent, reorder(scan_orders[0]), reorder(scan_orders[1])])
    upstream = jnp.einsum(
        "ovtd,odi->ovti",
        scanned,
        lax.all_gather(out_weight, "ctx", axis=1, tiled=True),
        preferred_element_type=jnp.float32,
    ).astype(jnp.bfloat16)
    upstream = lax.optimization_barrier(upstream)
    signal = head_inputs.astype(jnp.float32).reshape(3, volumes, tokens, local_heads, P_SIZE)
    grad_up = upstream.astype(jnp.float32).reshape(3, volumes, tokens, local_heads, P_SIZE)
    writes = write_read[..., :N].astype(jnp.float32)
    readers = write_read[..., N:].astype(jnp.float32)
    log_rates = -decay_steps.astype(jnp.float32) / seq_len
    running = jnp.cumsum(log_rates, axis=-1)
    summed_log = running[..., -1]
    end_state = contract(
        "ovht,ovtn,ovthp->ovhnp", jnp.exp(summed_log[..., None] - running), writes, signal
    )
    start_grad = contract("ovht,ovtn,ovthp->ovhnp", jnp.exp(running), readers, grad_up)
    zeros_log = jnp.zeros_like(summed_log)
    zeros_state = jnp.zeros_like(end_state)
    _, state_in = prefix(
        (summed_log, end_state), "ctx", carry_forward, (zeros_log, zeros_state), False
    )
    _, grad_out = prefix(
        (summed_log, start_grad), "ctx", carry_backward, (zeros_log, zeros_state), True
    )
    length = math.gcd(tokens, 128)
    outputs, grad_signal, grad_writes, grad_readers = run_segments(
        signal, writes, readers, log_rates, grad_up, state_in, grad_out, length
    )
    grad_wr = lax.psum(jnp.concatenate([grad_writes, grad_readers], axis=-1), "mp").astype(
        jnp.bfloat16
    )
    grad_inputs = grad_signal.reshape(3, volumes, tokens, inner_width).astype(jnp.bfloat16)
    outputs_bf = outputs.reshape(3, volumes, tokens, inner_width).astype(jnp.bfloat16)
    weight_term = jnp.einsum(
        "ovtd,ovti->odi", scanned, outputs_bf, preferred_element_type=jnp.float32
    )
    rows_sum = lax.psum_scatter(weight_term, "ctx", scatter_dimension=1, tiled=True)
    weight_grad = lax.psum(rows_sum, "dp").astype(jnp.bfloat16)
    return (grad_inputs, grad_wr, weight_grad)


def solution(mesh):
    in_specs = (
        P(None, ("groups", "dp"), "ctx", "mp"),
        P(None, ("groups", "dp"), "ctx", None),
        P(None, ("groups", "dp"), "mp", "ctx"),
        P(None, ("groups", "dp"), "ctx"),
        P(("groups", "dp"), "ctx", None),
        P(None, "ctx", "mp"),
    )
    out_specs = (
        P(None, ("groups", "dp"), "ctx", "mp"),
        P(None, ("groups", "dp"), "ctx", None),
        P("groups", "ctx", "mp"),
    )
    return jax.shard_map(shards, mesh=mesh, in_specs=in_specs, out_specs=out_specs, check_vma=False)
```

profile of v0, /device:TPU:0, one launch (start us, length us, event | category | flops | bytes accessed | tf_op | source)
XLA Modules:
  0.0 406.5 jit_solution(13065868097995965039)
XLA Ops:
  8.0 0.7 fusion.84
  8.7 5.4 %reduce-window.6 = f32[3,1,6,2,128]{4,3,2,1,0:T(2,128)S(1)} reduce-window(f32[3,1,6,2,128]{4,3,2,1,0:T(2,128)S(1)} %bitcast.295, f32[]{:T(128)} %constant.173.clone.1), window={size=1x1x1x1x128 pad=0_0x0_0x0_0x0_0x127_0}, to_apply=%region_0.0 | reduce-window | flops 585216 | bytes 36868 | tf_op jit(solution)/shard_map/reduce-window
  14.6 1.1 fusion.94
  17.6 0.8 convert_bitcast_fusion.1
  18.4 2.2 fusion.72
  21.5 1.7 copy.120
  23.2 14.1 %all-gather.1 = f32[12,1,6,1]{2,3,1,0:T(1,128)} all-gather(f32[3,1,6,1]{2,3,1,0:T(1,128)S(1)} %copy.107), channel_id=3, replica_groups=mesh['groups'=2,'ctx'=4,'dp'=2,'mp'=2] {'ctx'}, dimensions={0}, use_global_device_ids=true | all-gather | bytes 360 | tf_op jit(solution)/shard_map/all_gather | solution.py:14
  37.3 12.2 %all-gather.8.cloned.1.call-done = bf16[1,1024,768]{2,1,0:T(8,128)(2,1)} async-done(((bf16[1,256,768]{2,1,0:T(8,128)(2,1)}), bf16[1,1024,768]{2,1,0:T(8,128)(2,1)}) %all-gather.8.cloned.1.call-update) | async-done | bytes 1572880 | tf_op jit(solution)/shard_map/all_gather | solution.py:143
  49.6 3.6 gather_fusion
  53.2 2.9 gather_fusion.1
  56.1 45.0 %all-gather.14.cloned.1.call-done = f32[12,6,64,128]{3,2,1,0:T(8,128)} async-done(((f32[3,6,64,128]{3,2,1,0:T(8,128)}), f32[12,6,64,128]{3,2,1,0:T(8,128)}) %all-gather.14.cloned.1.call-update) | async-done | bytes 2359312 | tf_op jit(solution)/shard_map/all_gather | solution.py:14
  101.1 5.7 %while.69 = (s32[]{:T(128)}, f32[3,1,6,64,128]{4,3,2,1,0:T(8,128)S(1)}, s32[]{:T(128)}, f32[4,3,1,6]{3,2,1,0:T(1,128)}, f32[4,3,1,6,64,128]{5,4,3,1,2,0:T(8,128)}, /*index=5*/s32[]{:T(128)}, s32[]{:T(128)}) while((s32[]{:T(128)}, f32[3,1,6,64,128]{4,3,2,1,0:T(8,128)S(1)}, s32[]{:T(128)}, f32[4,3,1,6]{3,2,1,0:T(1,128)}, ...), condition=%wide.region_5.6_spmd.clone, body=%wide.region_4.5_spmd.clone.sunk | while | flops 589828 | bytes 1769937 | solution.py:26
  101.8 1.2 fusion.187
  103.7 1.2 fusion.187
  105.6 1.2 fusion.187
  106.8 64.7 %all-gather.10.cloned.1.call-done = bf16[3,768,768]{2,1,0:T(8,128)(2,1)} async-done(((bf16[3,192,768]{2,1,0:T(8,128)(2,1)}), bf16[3,768,768]{2,1,0:T(8,128)(2,1)}) %all-gather.10.cloned.1.call-update) | async-done | bytes 3538960 | tf_op jit(solution)/shard_map/all_gather | solution.py:152
  171.5 3.3 fusion.71
  174.8 1.5 copy.104
  176.3 3.5 fusion.74
  180.2 27.0 %while.66 = (s32[]{:T(128)}, f32[3,1,6,64,128]{4,3,2,0,1:T(8,128)S(1)}, bf16[3,1,256,6,128]{2,4,3,0,1:T(8,128)(2,1)S(1)}, f32[2,3,1,6,64,128]{5,4,3,1,2,0:T(8,12...) while((s32[]{:T(128)}, ...), condition=%wide.region_8.9_spmd, body=%wide.region_6.8_spmd.sunk | while | flops 946094080 | bytes 10168943 | solution.py:99
  180.2 1.3 constant_dynamic-slice_fusion.10
  181.5 1.9 reduce_window_sum.68
  183.7 0.9 dynamic-slice_bitcast_fusion.6
  184.6 2.0 convolution_bitcast_fusion.8
  187.1 3.9 fusion.159
  191.2 2.5 fusion.157
  193.7 1.3 constant_dynamic-slice_fusion.10
  195.0 1.9 reduce_window_sum.68
  197.2 0.9 dynamic-slice_bitcast_fusion.6
  198.1 2.0 convolution_bitcast_fusion.8
  200.6 3.9 fusion.159
  204.6 2.5 fusion.157
  207.2 5.7 %fusion.82 = f32[3,768,768]{2,1,0:T(8,128)} fusion(bf16[3,256,768]{1,2,0:T(8,128)(2,1)S(1)} %bitcast.282, bf16[1,1,256,768]{3,2,0,1:T(8,128)(2,1)} %bitcast.290, bf16[1,1,256,768]{3,2,0,1:T(8,128)(2,1)S(1)} %bitcast.288, bf16[1,1,256,768]{3,2,0,1:T(8,128)(2,1)} %bitcast.292), kind=kOutput, calls=%fused_computation.120 | convolution fusion | flops 907149312 | bytes 9437184 | tf_op jit(solution)/shard_map/ovtd,ovti->odi/dot_general | solution.py:184
  214.2 1.8 copy.109
  216.0 13.1 %all-gather.12.cloned.1.call-done = f32[12,6,64,128]{3,2,1,0:T(8,128)} async-done(((f32[3,6,64,128]{3,2,1,0:T(8,128)}), f32[12,6,64,128]{3,2,1,0:T(8,128)}) %all-gather.12.cloned.1.call-update) | async-done | bytes 2359312 | tf_op jit(solution)/shard_map/all_gather | solution.py:14
  229.1 1.8 rev.6
  231.7 0.7 broadcast.217
  233.1 41.1 %while.67 = (s32[]{:T(128)}, f32[3,1,6,64,128]{4,3,2,0,1:T(8,128)S(1)}, bf16[3,1,256,6,128]{2,4,3,0,1:T(8,128)(2,1)S(1)}, f32[3,1,256,64]{2,3,0,1:T(8,128)}, f32...) while((s32[]{:T(128)}, ...), condition=%wide.region_12.13_spmd, body=%wide.region_9.12_spmd.sunk | while | flops 1929625600 | bytes 41488220 | solution.py:120
  233.1 0.9 reduce_window_sum.69
  234.1 1.1 dynamic-slice_bitcast_fusion.7
  235.2 2.0 convolution_bitcast_fusion.9
  237.9 1.7 fusion.178
  239.6 1.0 copy-done.5
  241.0 2.3 fusion.182
  243.3 3.7 fusion.180
  247.5 2.6 fusion.179
  250.2 2.4 fusion.176
  252.6 0.9 fusion.181
  253.6 0.8 reduce_window_sum.69
  254.6 1.1 dynamic-slice_bitcast_fusion.7
  255.7 2.0 convolution_bitcast_fusion.9
  258.4 1.7 fusion.178
  260.1 1.0 copy-done.5
  261.5 2.3 fusion.182
  263.8 3.7 fusion.180
  268.0 2.7 fusion.179
  270.7 2.4 fusion.176
  273.2 0.9 fusion.181
  274.1 1.1 copy.121
  275.2 1.1 copy.122
  276.5 1.5 copy.125
  278.0 5.0 %all-reduce.2 = bf16[3,1,256,128]{3,2,1,0:T(8,128)(2,1)} all-reduce(f32[3,1,256,128]{3,2,1,0:T(8,128)S(1)} %pad_maximum_fusion), channel_id=1, replica_groups=mesh['groups'=2,'ctx'=4,'dp'=2,'mp'=2] {'mp'}, use_global_device_ids=true, to_apply=%region_13.14 | all-reduce | flops 98304 | bytes 589824 | tf_op jit(solution)/shard_map/psum | solution.py:179
  283.0 70.6 %reduce-scatter.2.cloned.1.call-done = f32[3,192,768]{2,1,0:T(8,128)} async-done(((f32[3,768,768]{2,1,0:T(8,128)}), f32[3,192,768]{2,1,0:T(8,128)}) %reduce-scatter.2.cloned.1.call-update) | async-done | bytes 1769488 | tf_op jit(solution)/shard_map/reduce_scatter | solution.py:187
  353.6 46.3 %all-reduce.3 = bf16[3,192,768]{2,1,0:T(8,128)(2,1)} all-reduce(f32[3,192,768]{2,1,0:T(8,128)} %reduce-scatter.2.cloned.1.call-done), channel_id=1, replica_groups=mesh['groups'=2,'ctx'=4,'dp'=2,'mp'=2] {'dp'}, use_global_device_ids=true, to_apply=%region_15.16 | all-reduce | flops 442368 | bytes 2654208 | tf_op jit(solution)/shard_map/psum | solution.py:188
  (121 shorter events, 14.7 us)
Async XLA Ops:
  7.2 8.9 %copy-start.10 = (bf16[3,1,256,768]{3,2,1,0:T(8,128)(2,1)S(1)}, bf16[3,1,256,768]{3,2,1,0:T(8,128)(2,1)}, u32[]{:S(2)}) copy-start(bf16[3,1,256,768]{3,2,1,0:T(8,128)(2,1)} %param.14) | copy-start | bytes 3538948
  7.2 42.4 %all-gather.8.cloned.1.call-start = ((), (), s32[]{:S(2)}) async-start(), calls=%async_computation.1 | async-start | bytes 1966080 | tf_op jit(solution)/shard_map/all_gather | solution.py:143
  7.9 93.2 %all-gather.14.cloned.1.call-start = ((), (), s32[]{:S(2)}) async-start(), calls=%async_computation.5 | async-start | bytes 2949120 | tf_op jit(solution)/shard_map/all_gather | solution.py:14
  8.7 8.0 %copy-start.8 = (f32[3,1,6,256]{3,2,1,0:T(8,128)}, f32[3,1,6,256]{3,2,1,0:T(8,128)S(1)}, u32[]{:S(2)}) copy-start(f32[3,1,6,256]{3,2,1,0:T(8,128)S(1)} %fusion.84) | copy-start | bytes 55300
  20.6 150.9 %all-gather.10.cloned.1.call-start = ((), (), s32[]{:S(2)}) async-start(), calls=%async_computation.2 | async-start | bytes 4423680 | tf_op jit(solution)/shard_map/all_gather | solution.py:152
  21.3 207.8 %all-gather.12.cloned.1.call-start = ((), (), s32[]{:S(2)}) async-start(), calls=%async_computation.4 | async-start | bytes 2949120 | tf_op jit(solution)/shard_map/all_gather | solution.py:14
  21.5 15.8 %copy-start.14 = (s32[2,1,256]{2,1,0:T(1,128)S(1)}, s32[2,1,256]{2,1,0:T(1,128)}, u32[]{:S(2)}) copy-start(s32[2,1,256]{2,1,0:T(1,128)} %param.17) | copy-start | bytes 6148
  49.6 3.7 copy-start.1
  101.1 70.4 %copy-start.7 = (bf16[256,768]{1,0:T(8,128)(2,1)S(1)}, bf16[256,768]{1,0:T(8,128)(2,1)}, u32[]{:S(2)}) copy-start(bf16[256,768]{1,0:T(8,128)(2,1)} %gather_fusion) | copy-start | bytes 1179652
  174.8 1.5 copy-start.3
  179.8 173.8 %reduce-scatter.2.cloned.1.call-start = ((), (), s32[]{:S(2)}) async-start(), calls=%async_computation.3 | async-start | bytes 8847360 | tf_op jit(solution)/shard_map/reduce_scatter | solution.py:187
  207.2 5.8 %copy-start.2 = (f32[2,3,1,6,64,128]{5,4,3,1,2,0:T(8,128)}, f32[2,3,1,6,64,128]{5,4,3,1,2,0:T(8,128)S(1)}, u32[]{:S(2)}) copy-start(f32[2,3,1,6,64,128]{5,4,3,1,2,0:T(8,128)S(1)} %get-tuple-element.1132) | copy-start | bytes 3538948
  212.9 0.7 copy-start.13
  212.9 1.3 copy-start.4
  231.5 1.5 copy-start.9
  234.1 3.6 copy-start
  239.6 1.0 copy-start.5
  243.3 3.7 copy-start.11
  247.5 2.6 copy-start.12
  250.2 3.4 copy-start.6
  254.6 3.6 copy-start
  260.1 1.0 copy-start.5
  263.8 3.7 copy-start.11
  268.0 2.7 copy-start.12
  270.7 3.4 copy-start.6
Sparse Core Ops, SparseCore 0:
  9.6 39.9 all-gather.7
  51.7 49.3 all-gather.13
  102.7 68.7 all-gather.9
  180.0 49.1 all-gather.11
  231.3 122.3 reduce-scatter.1
where the time goes:
time: 408 us; the launch traced here: 406 us
  waiting for transfers between devices  207 us (51%)
  matrix products  66.1 us (16%)
  blocking collectives  65.4 us (16%)
  local copies, waits for them, and re-layouts  35.1 us (9%)
  other arithmetic  18 us (4%)
  between operations  14 us (3%)
    reduce_scatter x1, waiting for transfers between devices, shards(): lax.psum_scatter(weight_term, 'ctx', scatter_dimension=1, tiled=True)  70.6 us
    all_gather x1, waiting for transfers between devices, shards(): lax.all_gather(out_weight, 'ctx', axis=1, tiled=True)  64.7 us
    all_gather x2, waiting for transfers between devices, prefix(): pieces = jax.tree.map(lambda part: lax.all_gather(part, axis), value)  58.1 us
    dot_general x28, matrix products, contract(): return jnp.einsum(form, *operands, precision=EXACT)  57 us
    psum x1, blocking collectives, shards(): weight_grad = lax.psum(rows_sum, 'dp').astype(jnp.bfloat16)  46.3 us
    all_gather x1, blocking collectives, prefix(): pieces = jax.tree.map(lambda part: lax.all_gather(part, axis), value)  14.1 us
    all_gather x1, waiting for transfers between devices, shards(): gathered = lax.all_gather(cotangent, 'ctx', axis=1, tiled=True)  12.2 us
  transfers between devices with their start and end apart: 5, of which 5 were waited for; matrix products, arithmetic and copies ran while one was open for 26% of the time, Pallas kernels for 0%

commit v1 on v0

--- a/solution.py
+++ b/solution.py
@@ -7,6 +7,22 @@
 P_SIZE = 128
 N = 64
 EXACT = lax.Precision.HIGHEST
+
+
+def summed_both_ways(x, axis, dim, term):
+    count, index, extent = (lax.axis_size(axis), lax.axis_index(axis), x.shape[dim])
+    right = [(i, (i + 1) % count) for i in range(count)]
+    left = [(i, (i - 1) % count) for i in range(count)]
+    halfway = count // 2
+    from_left = from_right = x
+    running = term(x, index * extent)
+    for hop in range(1, halfway + 1):
+        from_left = lax.ppermute(from_left, axis, right)
+        if hop < count - halfway:
+            from_right = lax.ppermute(from_right, axis, left)
+            running = running + term(from_right, (index + hop) % count * extent)
+        running = running + term(from_left, (index - hop) % count * extent)
+    return running
 
 
 def prefix(value, axis, join, neutral, backward):
@@ -146,11 +162,16 @@
         return jax.vmap(lambda table_rows, row_ids: table_rows[row_ids])(gathered, ordering)
 
     scanned = jnp.stack([cotangent, reorder(scan_orders[0]), reorder(scan_orders[1])])
-    upstream = jnp.einsum(
-        "ovtd,odi->ovti",
-        scanned,
-        lax.all_gather(out_weight, "ctx", axis=1, tiled=True),
-        preferred_element_type=jnp.float32,
+    upstream = summed_both_ways(
+        out_weight,
+        "ctx",
+        1,
+        lambda own_block, at: jnp.einsum(
+            "ovtd,odi->ovti",
+            lax.dynamic_slice_in_dim(scanned, at, own_block.shape[1], axis=3),
+            own_block,
+            preferred_element_type=jnp.float32,
+        ),
     ).astype(jnp.bfloat16)
     upstream = lax.optimization_barrier(upstream)
     signal = head_inputs.astype(jnp.float32).reshape(3, volumes, tokens, local_heads, P_SIZE)

time: 408 us -> 383 us (0.939)
  waiting for transfers between devices: 207 us -> 116 us
  blocking collectives: 65.4 us -> 117 us
  starting transfers between devices: 0.38 us -> 5.57 us
  local copies, waits for them, and re-layouts: 35.1 us -> 39.5 us
    all_gather x1 -> x0, waiting for transfers between devices: 64.7 us -> none  [shards(): lax.all_gather(out_weight, 'ctx', axis=1, tiled=True)]
    all_gather x1, blocking collectives: 14.1 us -> 65.2 us  [prefix(): pieces = jax.tree.map(lambda part: lax.all_gather(part, axis), value)]
    all_gather x2, waiting for transfers between devices: 58.1 us -> 18.3 us  [prefix(): pieces = jax.tree.map(lambda part: lax.all_gather(part, axis), value)]
    ppermute x0 -> x3, waiting for transfers between devices: none -> 26.3 us  [the longest x2 26.3 us: summed_both_ways(): from_left = lax.ppermute(from_left, axis, right)]
    all_gather x1, waiting for transfers between devices: 12.2 us -> 0.02 us  [shards(): gathered = lax.all_gather(cotangent, 'ctx', axis=1, tiled=True)]
    ppermute x0 -> x3, starting transfers between devices: none -> 5.23 us  [the longest x2 3.14 us: summed_both_ways(): from_left = lax.ppermute(from_left, axis, right)]
    gather x3 -> x6, local copies, waits for them, and re-layouts: 6.56 us -> 9.64 us  [reorder(): table_rows[row_ids]]
  transfers between devices with their start and end apart: 5 -> 7, of which waited for: 5 -> 4; matrix products, arithmetic and copies ran while one was open for 26% -> 32% of each run, Pallas kernels for 0% -> 0%
where the time goes in v1:
time: 383 us; the launch traced here: 381 us
  blocking collectives  117 us (31%)
  waiting for transfers between devices  116 us (30%)
  matrix products  69.7 us (18%)
  local copies, waits for them, and re-layouts  39.5 us (10%)
  other arithmetic  19.4 us (5%)
  between operations  14 us (4%)
  starting transfers between devices  5.57 us (1%)
    reduce_scatter x1, waiting for transfers between devices, shards(): lax.psum_scatter(weight_term, 'ctx', scatter_dimension=1, tiled=True)  70.6 us
    all_gather x1, blocking collectives, prefix(): pieces = jax.tree.map(lambda part: lax.all_gather(part, axis), value)  65.2 us
    dot_general x28, matrix products, contract(): return jnp.einsum(form, *operands, precision=EXACT)  56.9 us
    psum x1, blocking collectives, shards(): weight_grad = lax.psum(rows_sum, 'dp').astype(jnp.bfloat16)  46.4 us
    ppermute x2, waiting for transfers between devices, summed_both_ways(): from_left = lax.ppermute(from_left, axis, right)  26.3 us
    all_gather x2, waiting for transfers between devices, prefix(): pieces = jax.tree.map(lambda part: lax.all_gather(part, axis), value)  18.3 us
    gather x6, local copies, waits for them, and re-layouts, reorder(): table_rows[row_ids]  9.64 us
  transfers between devices with their start and end apart: 7, of which 4 were waited for; matrix products, arithmetic and copies ran while one was open for 32% of the time, Pallas kernels for 0%

profile of v1, /device:TPU:0, one launch (start us, length us, event | category | flops | bytes accessed | tf_op | source)
XLA Modules:
  0.0 381.4 jit_solution(9599549985815741837)
XLA Ops:
  8.7 5.4 %reduce-window.6 = f32[3,1,6,2,128]{4,3,2,1,0:T(2,128)S(1)} reduce-window(f32[3,1,6,2,128]{4,3,2,1,0:T(2,128)S(1)} %bitcast.309, f32[]{:T(128)} %constant.197.clone.1), window={size=1x1x1x1x128 pad=0_0x0_0x0_0x0_0x127_0}, to_apply=%region_0.1 | reduce-window | flops 585216 | bytes 36868 | tf_op jit(solution)/shard_map/reduce-window
  14.6 1.1 fusion.108
  18.4 2.2 fusion.74
  20.6 3.1 collective-permute-start.1
  23.7 2.1 collective-permute-start
  26.8 1.8 copy.129
  28.6 65.2 %all-gather.1 = f32[12,1,6,1]{2,3,1,0:T(1,128)S(1)} all-gather(f32[3,1,6,1]{2,3,1,0:T(1,128)S(1)} %copy.116), channel_id=3, replica_groups=mesh['groups'=2,'ctx'=4,'dp'=2,'mp'=2] {'ctx'}, dimensions={0}, use_global_device_ids=true | all-gather | bytes 360 | tf_op jit(solution)/shard_map/all_gather | solution.py:30
  94.0 3.7 gather_fusion
  97.6 1.9 copy.111
  99.5 2.9 gather_fusion.1
  102.4 1.2 copy.112
  103.6 1.4 pad_maximum_fusion
  105.0 1.7 fusion.89
  106.7 1.7 fusion.85
  108.4 1.7 fusion.87
  110.1 26.3 %collective-permute-done.2 = bf16[3,192,768]{2,1,0:T(8,128)(2,1)} collective-permute-done((bf16[3,192,768]{2,1,0:T(8,128)(2,1)}, bf16[3,192,768]{2,1,0:T(8,128)(2,1)}, u32[]{:S(2)}, u32[]{:S(2)}) %collective-permute-start.2) | collective-permute-done | bytes 884768 | tf_op jit(solution)/shard_map/ppermute | solution.py:20
  136.5 1.8 fusion.71
  138.3 1.5 copy.113
  139.7 3.4 fusion.76
  143.4 5.0 %all-gather.11.cloned.1.call-done = f32[12,6,64,128]{3,2,1,0:T(8,128)} async-done(((f32[3,6,64,128]{3,2,1,0:T(8,128)}), f32[12,6,64,128]{3,2,1,0:T(8,128)}) %all-gather.11.cloned.1.call-update) | async-done | bytes 2359312 | tf_op jit(solution)/shard_map/all_gather | solution.py:30
  148.4 3.7 while.69
  148.4 1.2 fusion.204
  149.6 1.2 fusion.204
  150.9 1.2 fusion.204
  152.1 1.1 broadcast.219.clone
  153.3 28.9 %while.66 = (s32[]{:T(128)}, f32[3,1,6,64,128]{4,3,2,0,1:T(8,128)S(1)}, bf16[3,1,256,6,128]{2,4,3,0,1:T(8,128)(2,1)}, f32[2,3,1,6,64,128]{5,4,3,1,2,0:T(8,128)S(...) while((s32[]{:T(128)}, ...), condition=%wide.region_8.9_spmd, body=%wide.region_6.8_spmd.sunk | while | flops 946094080 | bytes 19606184 | solution.py:115
  153.3 1.4 constant_dynamic-slice_fusion.10
  154.6 1.9 reduce_window_sum.68
  157.7 2.0 convolution_bitcast_fusion.8
  160.3 4.0 %fusion.176 = bf16[3,1,256,6,128]{2,4,3,0,1:T(8,128)(2,1)S(1)} fusion(bf16[3,1,256,6,128]{2,4,3,0,1:T(8,128)(2,1)S(1)} %copy-done.3, s32[]{:T(128)S(6)} %select_n.245, f32[3,1,128,6,128]{2,4,3,0,1:T(8,128)S(1)} %convolution_bitcast_fusion.8, f32[3,1,256,6,128]{4,2,3,0,1:T(8,128)} %get-tuple-element.1115, f32[3,6,128]{2,1,0:T(8,128)S(1)} %bitcast.295, ...), kind=kOutput, calls=%fused_computation.15.clone.1 | convolution fusion | flops 454459392 | bytes 3777536 | tf_op jit(solution)/shard_map/while/body/eval_jaxpr/ovhij,ovjhp->ovihp/dot_general | solution.py:46
  165.3 2.5 fusion.174
  167.8 1.3 constant_dynamic-slice_fusion.10
  169.1 1.9 reduce_window_sum.68
  172.2 2.0 convolution_bitcast_fusion.8
  174.7 3.9 %fusion.176 = bf16[3,1,256,6,128]{2,4,3,0,1:T(8,128)(2,1)S(1)} fusion(bf16[3,1,256,6,128]{2,4,3,0,1:T(8,128)(2,1)S(1)} %copy-done.3, s32[]{:T(128)S(6)} %select_n.245, f32[3,1,128,6,128]{2,4,3,0,1:T(8,128)S(1)} %convolution_bitcast_fusion.8, f32[3,1,256,6,128]{4,2,3,0,1:T(8,128)} %get-tuple-element.1115, f32[3,6,128]{2,1,0:T(8,128)S(1)} %bitcast.295, ...), kind=kOutput, calls=%fused_computation.15.clone.1 | convolution fusion | flops 454459392 | bytes 3777536 | tf_op jit(solution)/shard_map/while/body/eval_jaxpr/ovhij,ovjhp->ovihp/dot_general | solution.py:46
  179.6 2.5 fusion.174
  182.2 6.0 %fusion.72 = f32[3,768,768]{2,1,0:T(8,128)} fusion(bf16[3,256,768]{1,2,0:T(8,128)(2,1)} %bitcast.296, bf16[1,1,256,768]{2,3,0,1:T(8,128)(2,1)} %bitcast.305, bf16[1,1,256,768]{2,3,0,1:T(8,128)(2,1)} %bitcast.303, bf16[1,1,256,768]{2,3,0,1:T(8,128)(2,1)S(1)} %bitcast.301), kind=kOutput, calls=%fused_computation.110 | convolution fusion | flops 907149312 | bytes 9437184 | tf_op jit(solution)/shard_map/ovtd,ovti->odi/dot_general | solution.py:205
  188.9 1.8 copy.118
  190.7 13.3 %all-gather.9.cloned.1.call-done = f32[12,6,64,128]{3,2,1,0:T(8,128)} async-done(((f32[3,6,64,128]{3,2,1,0:T(8,128)}), f32[12,6,64,128]{3,2,1,0:T(8,128)}) %all-gather.9.cloned.1.call-update) | async-done | bytes 2359312 | tf_op jit(solution)/shard_map/all_gather | solution.py:30
  204.0 1.8 rev.6
  207.9 41.1 %while.67 = (s32[]{:T(128)}, f32[3,1,6,64,128]{4,3,2,0,1:T(8,128)S(1)}, bf16[3,1,256,6,128]{2,4,3,0,1:T(8,128)(2,1)S(1)}, f32[3,1,256,64]{2,3,0,1:T(8,128)}, f32...) while((s32[]{:T(128)}, ...), condition=%wide.region_12.13_spmd, body=%wide.region_9.12_spmd.sunk | while | flops 1929625600 | bytes 41488220 | solution.py:136
  209.0 1.1 dynamic-slice_bitcast_fusion.7
  210.1 2.0 convolution_bitcast_fusion.9
  212.8 1.7 fusion.195
  214.5 1.0 copy-done.5
  215.9 2.3 fusion.199
  218.2 3.7 fusion.197
  222.4 2.6 fusion.196
  225.1 2.4 fusion.193
  227.5 0.9 fusion.198
  229.5 1.1 dynamic-slice_bitcast_fusion.7
  230.6 2.0 convolution_bitcast_fusion.9
  233.2 1.7 fusion.195
  235.0 1.0 copy-done.5
  236.4 2.3 fusion.199
  238.7 3.7 fusion.197
  242.9 2.7 fusion.196
  245.6 2.4 fusion.193
  249.0 1.1 copy.130
  250.1 1.1 copy.131
  251.4 1.5 copy.133
  252.9 5.0 %all-reduce.2 = bf16[3,1,256,128]{3,2,1,0:T(8,128)(2,1)} all-reduce(f32[3,1,256,128]{3,2,1,0:T(8,128)S(1)} %pad_maximum_fusion.1), channel_id=1, replica_groups=mesh['groups'=2,'ctx'=4,'dp'=2,'mp'=2] {'mp'}, use_global_device_ids=true, to_apply=%region_13.14 | all-reduce | flops 98304 | bytes 589824 | tf_op jit(solution)/shard_map/psum | solution.py:200
  257.9 70.6 %reduce-scatter.2.cloned.1.call-done = f32[3,192,768]{2,1,0:T(8,128)} async-done(((f32[3,768,768]{2,1,0:T(8,128)}), f32[3,192,768]{2,1,0:T(8,128)}) %reduce-scatter.2.cloned.1.call-update) | async-done | bytes 1769488 | tf_op jit(solution)/shard_map/reduce_scatter | solution.py:208
  328.5 46.4 %all-reduce.3 = bf16[3,192,768]{2,1,0:T(8,128)(2,1)} all-reduce(f32[3,192,768]{2,1,0:T(8,128)} %reduce-scatter.2.cloned.1.call-done), channel_id=1, replica_groups=mesh['groups'=2,'ctx'=4,'dp'=2,'mp'=2] {'dp'}, use_global_device_ids=true, to_apply=%region_15.16 | all-reduce | flops 442368 | bytes 2654208 | tf_op jit(solution)/shard_map/psum | solution.py:209
  (145 shorter events, 20.9 us)
Async XLA Ops:
  7.2 8.9 %copy-start.12 = (bf16[3,1,256,768]{3,2,1,0:T(8,128)(2,1)S(1)}, bf16[3,1,256,768]{3,2,1,0:T(8,128)(2,1)}, u32[]{:S(2)}) copy-start(bf16[3,1,256,768]{3,2,1,0:T(8,128)(2,1)} %param.14) | copy-start | bytes 3538948
  7.2 86.8 %all-gather.7.cloned.1.call-start = ((), (), s32[]{:S(2)}) async-start(), calls=%async_computation.1 | async-start | bytes 1966080 | tf_op jit(solution)/shard_map/all_gather | solution.py:159
  7.9 140.5 %all-gather.11.cloned.1.call-start = ((), (), s32[]{:S(2)}) async-start(), calls=%async_computation.4 | async-start | bytes 2949120 | tf_op jit(solution)/shard_map/all_gather | solution.py:30
  8.7 8.0 %copy-start.10 = (f32[3,1,6,256]{3,2,1,0:T(8,128)}, f32[3,1,6,256]{3,2,1,0:T(8,128)S(1)}, u32[]{:S(2)}) copy-start(f32[3,1,6,256]{3,2,1,0:T(8,128)S(1)} %fusion.96) | copy-start | bytes 55300
  18.4 7.4 %copy-start.9 = (bf16[1,256,768]{2,1,0:T(8,128)(2,1)S(1)}, bf16[1,256,768]{2,1,0:T(8,128)(2,1)}, u32[]{:S(2)}) copy-start(bf16[1,256,768]{2,1,0:T(8,128)(2,1)} %param.18) | copy-start | bytes 1179652
  20.6 183.4 %all-gather.9.cloned.1.call-start = ((), (), s32[]{:S(2)}) async-start(), calls=%async_computation.3 | async-start | bytes 2949120 | tf_op jit(solution)/shard_map/all_gather | solution.py:30
  20.6 73.2 %collective-permute-start.1 = (bf16[3,192,768]{2,1,0:T(8,128)(2,1)}, bf16[3,192,768]{2,1,0:T(8,128)(2,1)}, u32[]{:S(2)}, u32[]{:S(2)}) collective-permute-start(bf16[3,192,768]{2,1,0:T(8,128)(2,1)} %param.19), channel_id=1, source_target_pairs={{0,4},{4,8},{8,12},{12,0},{1,5},{5,9},{9,13},{13,1},{2,6},{6,10},{... | collective-permute-start | bytes 2654216 | tf_op jit(solution)/shard_map/ppermute | solution.py:20
  23.7 84.7 %collective-permute-start = (bf16[3,192,768]{2,1,0:T(8,128)(2,1)}, bf16[3,192,768]{2,1,0:T(8,128)(2,1)}, u32[]{:S(2)}, u32[]{:S(2)}) collective-permute-start(bf16[3,192,768]{2,1,0:T(8,128)(2,1)} %param.19), channel_id=1, source_target_pairs={{0,12},{4,0},{8,4},{12,8},{1,13},{5,1},{9,5},{13,9},{2,14},{6,2},{... | collective-permute-start | bytes 2654216 | tf_op jit(solution)/shard_map/ppermute | solution.py:22
  26.8 67.0 %copy-start.19 = (s32[2,1,256]{2,1,0:T(1,128)S(1)}, s32[2,1,256]{2,1,0:T(1,128)}, u32[]{:S(2)}) copy-start(s32[2,1,256]{2,1,0:T(1,128)} %param.17) | copy-start | bytes 6148
  93.8 42.6 %collective-permute-start.2 = (bf16[3,192,768]{2,1,0:T(8,128)(2,1)}, bf16[3,192,768]{2,1,0:T(8,128)(2,1)}, u32[]{:S(2)}, u32[]{:S(2)}) collective-permute-start(bf16[3,192,768]{2,1,0:T(8,128)(2,1)} %collective-permute-done.1), channel_id=1, source_target_pairs={{0,4},{4,8},{8,12},{12,0},{1,5},{5,9},{9,13},{13,1},{2,6},{6,10},{... | collective-permute-start | bytes 2654216 | tf_op jit(solution)/shard_map/ppermute | solution.py:20
  93.9 5.6 %copy-start.1 = (bf16[1,1024,768]{2,1,0:T(8,128)(2,1)S(1)}, bf16[1,1024,768]{2,1,0:T(8,128)(2,1)}, u32[]{:S(2)}) copy-start(bf16[1,1024,768]{2,1,0:T(8,128)(2,1)} %all-gather.7.cloned.1.call-done) | copy-start | bytes 4718596
  103.6 1.4 copy-start.8
  138.3 1.5 copy-start.15
  138.3 1.5 copy-start.16
  143.2 185.3 %reduce-scatter.2.cloned.1.call-start = ((), (), s32[]{:S(2)}) async-start(), calls=%async_computation.2 | async-start | bytes 8847360 | tf_op jit(solution)/shard_map/reduce_scatter | solution.py:208
  152.1 1.1 copy-start.17
  153.2 28.9 %copy-start.7 = (bf16[1,256,768]{1,2,0:T(8,128)(2,1)S(1)}, bf16[1,256,768]{1,2,0:T(8,128)(2,1)}, u32[]{:S(2)}) copy-start(bf16[1,256,768]{1,2,0:T(8,128)(2,1)} %copy.110) | copy-start | bytes 1179652
  157.7 2.6 copy-start.3
  164.2 1.0 copy-start.4
  172.2 2.6 copy-start.3
  178.6 1.0 copy-start.4
  182.2 6.0 %copy-start.2 = (f32[2,3,1,6,64,128]{5,4,3,1,2,0:T(8,128)}, f32[2,3,1,6,64,128]{5,4,3,1,2,0:T(8,128)S(1)}, u32[]{:S(2)}) copy-start(f32[2,3,1,6,64,128]{5,4,3,1,2,0:T(8,128)S(1)} %get-tuple-element.1132) | copy-start | bytes 3538948
  188.2 0.7 copy-start.18
  206.4 1.5 copy-start.11
  209.0 3.6 copy-start
  214.5 1.0 copy-start.5
  218.2 3.7 copy-start.13
  222.4 2.6 copy-start.14
  225.1 3.4 copy-start.6
  229.5 3.6 copy-start
  235.0 1.0 copy-start.5
  238.7 3.7 copy-start.13
  242.9 2.7 copy-start.14
  245.6 3.4 copy-start.6
Sparse Core Ops, SparseCore 0:
  9.6 69.8 all-gather.6
  81.0 67.2 all-gather.10
  150.5 53.4 all-gather.8
  206.2 122.3 reduce-scatter.1
